TPU v7x, 32 devices: a whole 2x2x4 slice. The times are simulated.
32 devices in a mesh: tm: 4 (over y, core), space: 8 (over z, x).
Axes of the slice: x: 2, y: 2, z: 4, core: 2. Of those that a mesh axis runs over, the one named last changes fastest.
Arguments:
- init_states: float32 [2, 4, 256, 16, 128], P(None, 'tm', None, 'space'), may hold values from -6 to 6
- forcing: float32 [2, 256, 16, 128], P(None, None, 'space'), may hold values from -6 to 6
- damp: float32 [2, 256, 16, 128], P(None, None, 'space'), may hold values from 0.3 to 0.95
- kappa_x: float32 [256], replicated, may hold values from 2 to 60
- kappa_y: float32 [16], replicated, may hold values from 2 to 60
- kappa_z: float32 [128], replicated, may hold values from 0.02 to 0.24
- sea_tiles: int32 [16, 1], replicated, may hold values 0 or 1
- phases: int32 [4], P('tm'), may hold values from 0 to 11
Outputs:
- slab_starts: float32 [2, 4, 256, 16, 128], P(None, 'tm', None, 'space')
All inputs are finite; a program needn't handle non-finite values.
Results may differ from a plain program's by a relative error of at most 0.0003.
Values sent between devices are 32-bit elements; how exact they have to be, the bound alone decides.
A program may use at most 64 MiB of HBM per device.

v0:
```python
import math

import jax
import jax.numpy as jnp
from jax import lax
from jax.sharding import PartitionSpec as P

STEPS = 2
ITERS = 2
TILE = 16
PHASES = 12


def shifted(array, axis, by):
    devices = lax.axis_size(axis)
    return lax.ppermute(array, axis, [(i, (i + by) % devices) for i in range(devices)])


def line_inverse(kappa):
    face = 0.5 * (kappa[1:] + kappa[:-1])
    zero = jnp.zeros((1,), kappa.dtype)
    left = jnp.concatenate([zero, face])
    right = jnp.concatenate([face, zero])
    identity = jnp.eye(kappa.shape[0], dtype=kappa.dtype)
    return lax.linalg.tridiagonal_solve(-left, 1.0 + left + right, -right, identity)


def solve_lines(field, inverse):
    return jnp.matmul(inverse, field, precision=lax.Precision.HIGHEST)


def solve_x(field, inverse):
    shape = field.shape
    flat = field.reshape(shape[0], shape[1], shape[2], shape[3] * shape[4])
    return solve_lines(flat, inverse).reshape(shape)


def vertical_mix(field, kappa_z):
    face = 0.5 * (kappa_z[1:] + kappa_z[:-1])
    flux = face * (field[..., 1:] - field[..., :-1])
    zeros = jnp.zeros(field.shape[:-1] + (1,), field.dtype)
    flux = jnp.concatenate([zeros, flux, zeros], axis=-1)
    return field + flux[..., 1:] - flux[..., :-1]


def compose(earlier, later):
    return (earlier[0] * later[0], later[0] * earlier[1] + later[1])


def column_pass(field, inverse_y):
    return lax.all_to_all(
        solve_lines(
            lax.all_to_all(field, "space", split_axis=2, concat_axis=3, tiled=True), inverse_y
        ),
        "space",
        split_axis=3,
        concat_axis=2,
        tiled=True,
    )


def body(init_states, forcing, damp, kappa_x, kappa_y, kappa_z, sea_tiles, phases):
    row_count = init_states.shape[3]
    inverse_x = line_inverse(kappa_x)
    inverse_y = line_inverse(kappa_y)
    tiles = sea_tiles.astype(jnp.float32)
    sea = jnp.repeat(jnp.repeat(tiles, TILE, axis=0), TILE, axis=1)
    sea_rows = lax.dynamic_slice_in_dim(sea, lax.axis_index("space") * row_count, row_count, 1)
    source = (forcing * sea_rows[None, :, :, None])[:, None]
    phase_float = phases.astype(jnp.float32)
    weight = 1.0 + 0.5 * jnp.cos(2.0 * math.pi * phase_float / PHASES)
    factors = jnp.exp(weight[None, :, None, None, None] * jnp.log(damp)[:, None])
    states = init_states
    for iteration in range(ITERS):
        field = states
        for step in range(STEPS):
            amplitude = jnp.cos(2.0 * math.pi * (phase_float * STEPS + step) / (PHASES * STEPS))[
                None, :, None, None, None
            ]
            if step % 2 == 0:
                field = column_pass(solve_x(field, inverse_x), inverse_y)
            else:
                field = solve_x(column_pass(field, inverse_y), inverse_x)
            field = vertical_mix(field, kappa_z) + amplitude * source
        offsets = field - factors * states
        own_factor = factors[:, 0]
        own_offset = offsets[:, 0]
        own = (own_factor, own_offset)
        ident = (jnp.ones_like(own_factor), jnp.zeros_like(own_offset))
        count = lax.axis_size("tm")
        here = lax.axis_index("tm")
        lower_part = ident
        upper_part = ident
        moving = jnp.stack([own_factor, own_offset])
        for turn in range(1, count):
            moving = shifted(moving, "tm", 1)
            piece = (moving[0], moving[1])
            anchor = (here - turn) % count
            before = anchor < here
            joined_low = compose(piece, lower_part)
            joined_high = compose(piece, upper_part)
            lower_part = (
                jnp.where(before, joined_low[0], lower_part[0]),
                jnp.where(before, joined_low[1], lower_part[1]),
            )
            upper_part = (
                jnp.where(before, upper_part[0], joined_high[0]),
                jnp.where(before, upper_part[1], joined_high[1]),
            )
        period = compose(compose(lower_part, own), upper_part)
        first = period[1] / (1.0 - period[0])
        start = lower_part[0] * first + lower_part[1]
        fresh = [start]
        states = jnp.stack(fresh, axis=1)
    return states


def solution(mesh):
    return jax.shard_map(
        body,
        mesh=mesh,
        in_specs=(
            P(None, "tm", None, "space", None),
            P(None, None, "space", None),
            P(None, None, "space", None),
            P(),
            P(),
            P(),
            P(),
            P("tm"),
        ),
        out_specs=P(None, "tm", None, "space", None),
        check_vma=False,
    )
```

profile of v0, /device:TPU:0, one launch (start us, length us, event | category | flops | bytes accessed | tf_op | source)
XLA Modules:
  0.0 1152.5 jit_solution(6738022454229379222)
XLA Ops:
  7.5 593.1 %while.32 = (s32[]{:T(128)}, f32[]{:T(128)}, f32[256]{0:T(256)S(1)}, f32[7,32]{1,0:T(8,128)S(1)}, f32[7,32,256]{2,1,0:T(8,128)S(1)}, /*index=5*/f32[7,32]{1,0:T(...) while((s32[]{:T(128)}, f32[]{:T(128)}, ...), condition=%wide.region_1.2_spmd, body=%wide.region_0.1_spmd.sunk | while | flops 24705 | bytes 269565 | solution.py:25
  71.9 20.1 %subtract_divide_fusion.125 = (f32[256]{0:T(256)S(1)}, f32[256]{0:T(256)S(1)}, f32[256]{0:T(256)S(1)}, f32[256]{0:T(256)S(1)}, f32[256]{0:T(256)S(1)}, /*index=5...) fusion(f32[256]{0:T(256)S(1)} %bitcast.1625, ...), kind=kLoop, calls=%fused_computation.36.clone.1 | loop fusion | flops 24576 | bytes 66816 | tf_op jit(solution)/shard_map/while/body/eval_jaxpr/div | solution.py:25
  156.6 20.1 %subtract_divide_fusion.125 = (f32[256]{0:T(256)S(1)}, f32[256]{0:T(256)S(1)}, f32[256]{0:T(256)S(1)}, f32[256]{0:T(256)S(1)}, f32[256]{0:T(256)S(1)}, /*index=5...) fusion(f32[256]{0:T(256)S(1)} %bitcast.1625, ...), kind=kLoop, calls=%fused_computation.36.clone.1 | loop fusion | flops 24576 | bytes 66816 | tf_op jit(solution)/shard_map/while/body/eval_jaxpr/div | solution.py:25
  241.4 20.1 %subtract_divide_fusion.125 = (f32[256]{0:T(256)S(1)}, f32[256]{0:T(256)S(1)}, f32[256]{0:T(256)S(1)}, f32[256]{0:T(256)S(1)}, f32[256]{0:T(256)S(1)}, /*index=5...) fusion(f32[256]{0:T(256)S(1)} %bitcast.1625, ...), kind=kLoop, calls=%fused_computation.36.clone.1 | loop fusion | flops 24576 | bytes 66816 | tf_op jit(solution)/shard_map/while/body/eval_jaxpr/div | solution.py:25
  326.1 20.1 %subtract_divide_fusion.125 = (f32[256]{0:T(256)S(1)}, f32[256]{0:T(256)S(1)}, f32[256]{0:T(256)S(1)}, f32[256]{0:T(256)S(1)}, f32[256]{0:T(256)S(1)}, /*index=5...) fusion(f32[256]{0:T(256)S(1)} %bitcast.1625, ...), kind=kLoop, calls=%fused_computation.36.clone.1 | loop fusion | flops 24576 | bytes 66816 | tf_op jit(solution)/shard_map/while/body/eval_jaxpr/div | solution.py:25
  410.8 20.1 %subtract_divide_fusion.125 = (f32[256]{0:T(256)S(1)}, f32[256]{0:T(256)S(1)}, f32[256]{0:T(256)S(1)}, f32[256]{0:T(256)S(1)}, f32[256]{0:T(256)S(1)}, /*index=5...) fusion(f32[256]{0:T(256)S(1)} %bitcast.1625, ...), kind=kLoop, calls=%fused_computation.36.clone.1 | loop fusion | flops 24576 | bytes 66816 | tf_op jit(solution)/shard_map/while/body/eval_jaxpr/div | solution.py:25
  495.5 20.1 %subtract_divide_fusion.125 = (f32[256]{0:T(256)S(1)}, f32[256]{0:T(256)S(1)}, f32[256]{0:T(256)S(1)}, f32[256]{0:T(256)S(1)}, f32[256]{0:T(256)S(1)}, /*index=5...) fusion(f32[256]{0:T(256)S(1)} %bitcast.1625, ...), kind=kLoop, calls=%fused_computation.36.clone.1 | loop fusion | flops 24576 | bytes 66816 | tf_op jit(solution)/shard_map/while/body/eval_jaxpr/div | solution.py:25
  580.3 20.1 %subtract_divide_fusion.125 = (f32[256]{0:T(256)S(1)}, f32[256]{0:T(256)S(1)}, f32[256]{0:T(256)S(1)}, f32[256]{0:T(256)S(1)}, f32[256]{0:T(256)S(1)}, /*index=5...) fusion(f32[256]{0:T(256)S(1)} %bitcast.1625, ...), kind=kLoop, calls=%fused_computation.36.clone.1 | loop fusion | flops 24576 | bytes 66816 | tf_op jit(solution)/shard_map/while/body/eval_jaxpr/div | solution.py:25
  659.9 19.3 %subtract_divide_fusion.32 = (f32[256]{0:T(256)S(1)}, f32[256]{0:T(256)S(1)}, f32[256]{0:T(256)S(1)}, f32[256]{0:T(256)S(1)}, f32[256]{0:T(256)S(1)}, /*index=5*...) fusion(f32[256]{0:T(256)S(1)} %bitcast.1830, ...), kind=kLoop, calls=%fused_computation.288 | loop fusion | flops 23808 | bytes 64760 | tf_op jit(solution)/shard_map/eval_jaxpr/div | solution.py:25
  679.4 151.9 %while.33 = (s32[]{:T(128)}, f32[256]{0:T(256)S(1)}, f32[7,32,256]{2,1,0:T(8,128)S(1)}, f32[7,32,256]{2,1,0:T(8,128)S(1)}, f32[7,32]{1,0:T(8,128)S(1)}, /*index=...) while((s32[]{:T(128)}, f32[256]{0:T(256)S(1)}, ...), condition=%wide.region_3.4_spmd, body=%wide.region_2.3_spmd.sunk | while | flops 16418 | bytes 266713 | solution.py:25
  681.1 19.9 %multiply_subtract_fusion.154 = (f32[256]{0:T(256)S(1)}, f32[256]{0:T(256)S(1)}, f32[256]{0:T(256)S(1)}, f32[256]{0:T(256)S(1)}, f32[256]{0:T(256)S(1)}, /*index...) fusion(f32[256]{0:T(256)S(1)} %bitcast.1706, ...), kind=kLoop, calls=%fused_computation.102.clone.1 | loop fusion | flops 16384 | bytes 66688 | tf_op jit(solution)/shard_map/while/body/eval_jaxpr/sub | solution.py:25
  702.8 19.9 %multiply_subtract_fusion.154 = (f32[256]{0:T(256)S(1)}, f32[256]{0:T(256)S(1)}, f32[256]{0:T(256)S(1)}, f32[256]{0:T(256)S(1)}, f32[256]{0:T(256)S(1)}, /*index...) fusion(f32[256]{0:T(256)S(1)} %bitcast.1706, ...), kind=kLoop, calls=%fused_computation.102.clone.1 | loop fusion | flops 16384 | bytes 66688 | tf_op jit(solution)/shard_map/while/body/eval_jaxpr/sub | solution.py:25
  724.5 19.9 %multiply_subtract_fusion.154 = (f32[256]{0:T(256)S(1)}, f32[256]{0:T(256)S(1)}, f32[256]{0:T(256)S(1)}, f32[256]{0:T(256)S(1)}, f32[256]{0:T(256)S(1)}, /*index...) fusion(f32[256]{0:T(256)S(1)} %bitcast.1706, ...), kind=kLoop, calls=%fused_computation.102.clone.1 | loop fusion | flops 16384 | bytes 66688 | tf_op jit(solution)/shard_map/while/body/eval_jaxpr/sub | solution.py:25
  746.2 19.9 %multiply_subtract_fusion.154 = (f32[256]{0:T(256)S(1)}, f32[256]{0:T(256)S(1)}, f32[256]{0:T(256)S(1)}, f32[256]{0:T(256)S(1)}, f32[256]{0:T(256)S(1)}, /*index...) fusion(f32[256]{0:T(256)S(1)} %bitcast.1706, ...), kind=kLoop, calls=%fused_computation.102.clone.1 | loop fusion | flops 16384 | bytes 66688 | tf_op jit(solution)/shard_map/while/body/eval_jaxpr/sub | solution.py:25
  767.9 19.9 %multiply_subtract_fusion.154 = (f32[256]{0:T(256)S(1)}, f32[256]{0:T(256)S(1)}, f32[256]{0:T(256)S(1)}, f32[256]{0:T(256)S(1)}, f32[256]{0:T(256)S(1)}, /*index...) fusion(f32[256]{0:T(256)S(1)} %bitcast.1706, ...), kind=kLoop, calls=%fused_computation.102.clone.1 | loop fusion | flops 16384 | bytes 66688 | tf_op jit(solution)/shard_map/while/body/eval_jaxpr/sub | solution.py:25
  789.6 19.9 %multiply_subtract_fusion.154 = (f32[256]{0:T(256)S(1)}, f32[256]{0:T(256)S(1)}, f32[256]{0:T(256)S(1)}, f32[256]{0:T(256)S(1)}, f32[256]{0:T(256)S(1)}, /*index...) fusion(f32[256]{0:T(256)S(1)} %bitcast.1706, ...), kind=kLoop, calls=%fused_computation.102.clone.1 | loop fusion | flops 16384 | bytes 66688 | tf_op jit(solution)/shard_map/while/body/eval_jaxpr/sub | solution.py:25
  811.3 19.9 %multiply_subtract_fusion.154 = (f32[256]{0:T(256)S(1)}, f32[256]{0:T(256)S(1)}, f32[256]{0:T(256)S(1)}, f32[256]{0:T(256)S(1)}, f32[256]{0:T(256)S(1)}, /*index...) fusion(f32[256]{0:T(256)S(1)} %bitcast.1706, ...), kind=kLoop, calls=%fused_computation.102.clone.1 | loop fusion | flops 16384 | bytes 66688 | tf_op jit(solution)/shard_map/while/body/eval_jaxpr/sub | solution.py:25
  831.6 19.4 %multiply_subtract_fusion.32 = (f32[256]{0:T(256)S(1)}, f32[256]{0:T(256)S(1)}, f32[256]{0:T(256)S(1)}, f32[256]{0:T(256)S(1)}, f32[256]{0:T(256)S(1)}, /*index=...) fusion(f32[256]{0:T(256)S(1)} %bitcast.1799, ...), kind=kLoop, calls=%fused_computation.257 | loop fusion | flops 15872 | bytes 64636 | tf_op jit(solution)/shard_map/eval_jaxpr/sub | solution.py:25
  852.7 7.4 all-to-all-start
  891.2 9.2 fusion.49
  903.1 6.0 all-to-all-start.1
  911.2 11.9 %all-to-all-done.1 = f32[2,1,32,16,128]{4,2,0,1,3:T(8,128)S(1)} async-done(((f32[2,1,32,16,128]{4,2,0,1,3:T(8,128)}), f32[2,1,32,16,128]{4,2,0,1,3:T(8,128)S(1)}, u32[]{:S(2)}, u32[]{:S(2)}) %all-to-all-start.1) | async-done | bytes 524320 | tf_op jit(solution)/shard_map/all_to_all | solution.py:51
  924.8 17.6 %all_to_all.126 = f32[2,1,256,2,128]{4,3,0,1,2:T(2,128)S(1)} all-to-all(f32[2,1,256,2,128]{4,3,0,1,2:T(2,128)S(1)} %copy.234), channel_id=1, replica_groups=mesh['tm'=4,'space'=8] {'space'}, dimensions={2} | all-to-all | bytes 1048576 | tf_op jit(solution)/shard_map/all_to_all | solution.py:53
  944.1 3.7 all-to-all-start.3
  947.9 13.9 %all-to-all-done.3 = f32[2,1,32,16,128]{4,2,0,1,3:T(8,128)S(1)} async-done(((f32[2,1,32,16,128]{4,2,0,1,3:T(8,128)}), f32[2,1,32,16,128]{4,2,0,1,3:T(8,128)S(1)}, u32[]{:S(2)}, u32[]{:S(2)}) %all-to-all-start.3) | async-done | bytes 524320 | tf_op jit(solution)/shard_map/all_to_all | solution.py:51
  965.4 14.2 %collective-permute-done = f32[2,2,256,2,128]{4,2,3,1,0:T(8,128)S(1)} collective-permute-done((f32[2,2,256,2,128]{4,2,3,1,0:T(8,128)S(1)}, f32[2,2,256,2,128]{4,2,3,1,0:T(8,128)S(1)}, u32[]{:S(2)}, u32[]{:S(2)}) %collective-permute-start) | collective-permute-done | bytes 1048608 | tf_op jit(solution)/shard_map/ppermute | solution.py:16
  980.6 14.3 %collective-permute-done.1 = f32[2,2,256,2,128]{4,2,3,1,0:T(8,128)} collective-permute-done((f32[2,2,256,2,128]{4,2,3,1,0:T(8,128)S(1)}, f32[2,2,256,2,128]{4,2,3,1,0:T(8,128)}, u32[]{:S(2)}, u32[]{:S(2)}) %collective-permute-start.1) | collective-permute-done | bytes 1048608 | tf_op jit(solution)/shard_map/ppermute | solution.py:16
  997.0 2.2 slice_select_fusion.3
  1002.2 2.1 copy.250
  1004.2 2.1 fusion.90
  1006.3 2.1 copy.249
  1009.5 2.1 fusion.91
  1012.6 2.1 copy.243
  1014.8 2.8 fusion.3
  1019.2 19.3 %all_to_all.127 = f32[2,1,256,2,128]{4,3,0,1,2:T(2,128)S(1)} all-to-all(f32[2,1,256,2,128]{4,3,0,1,2:T(2,128)} %copy.253), channel_id=1, replica_groups=mesh['tm'=4,'space'=8] {'space'}, dimensions={2} | all-to-all | bytes 1048576 | tf_op jit(solution)/shard_map/all_to_all | solution.py:53
  1039.7 18.4 %all_to_all.128 = f32[2,1,32,16,128]{4,2,0,1,3:T(8,128)S(1)} all-to-all(f32[2,1,32,16,128]{4,2,0,1,3:T(8,128)S(1)} %copy.256), channel_id=1, replica_groups=mesh['tm'=4,'space'=8] {'space'}, dimensions={3} | all-to-all | bytes 1048576 | tf_op jit(solution)/shard_map/all_to_all | solution.py:51
  1059.1 17.6 %all_to_all.129 = f32[2,1,256,2,128]{4,3,0,1,2:T(2,128)S(1)} all-to-all(f32[2,1,256,2,128]{4,3,0,1,2:T(2,128)S(1)} %copy.258), channel_id=1, replica_groups=mesh['tm'=4,'space'=8] {'space'}, dimensions={2} | all-to-all | bytes 1048576 | tf_op jit(solution)/shard_map/all_to_all | solution.py:53
  1077.6 17.4 %all_to_all.130 = f32[2,1,32,16,128]{4,2,0,1,3:T(8,128)S(1)} all-to-all(f32[2,1,32,16,128]{4,2,0,1,3:T(8,128)S(1)} %copy.260), channel_id=1, replica_groups=mesh['tm'=4,'space'=8] {'space'}, dimensions={3} | all-to-all | bytes 1048576 | tf_op jit(solution)/shard_map/all_to_all | solution.py:51
  1095.4 1.2 reshape.738
  1096.6 2.0 fusion.34
  1100.7 1.2 copy.290
  1101.9 2.1 copy.289
  1104.0 1.2 subtract_multiply_fusion
  1105.5 2.3 bitcast_subtract_fusion
  1108.0 14.2 %collective-permute-done.3 = f32[2,2,256,2,128]{4,2,3,1,0:T(8,128)S(1)} collective-permute-done((f32[2,2,256,2,128]{4,2,3,1,0:T(8,128)S(1)}, f32[2,2,256,2,128]{4,2,3,1,0:T(8,128)S(1)}, u32[]{:S(2)}, u32[]{:S(2)}) %collective-permute-start.3) | collective-permute-done | bytes 1048608 | tf_op jit(solution)/shard_map/ppermute | solution.py:16
  1122.3 14.2 %collective-permute-done.4 = f32[2,2,256,2,128]{4,2,3,1,0:T(8,128)S(1)} collective-permute-done((f32[2,2,256,2,128]{4,2,3,1,0:T(8,128)S(1)}, f32[2,2,256,2,128]{4,2,3,1,0:T(8,128)S(1)}, u32[]{:S(2)}, u32[]{:S(2)}) %collective-permute-start.4) | collective-permute-done | bytes 1048608 | tf_op jit(solution)/shard_map/ppermute | solution.py:16
  1136.5 14.2 %collective-permute-done.5 = f32[2,2,256,2,128]{4,2,3,1,0:T(8,128)S(1)} collective-permute-done((f32[2,2,256,2,128]{4,2,3,1,0:T(8,128)S(1)}, f32[2,2,256,2,128]{4,2,3,1,0:T(8,128)S(1)}, u32[]{:S(2)}, u32[]{:S(2)}) %collective-permute-start.5) | collective-permute-done | bytes 1048608 | tf_op jit(solution)/shard_map/ppermute | solution.py:16
  1151.3 1.2 copy.283
  (285 shorter events, 85.1 us)
Async XLA Ops:
  0.0 0.7 copy-start.9
  679.4 151.9 %copy-start.4 = (f32[2,1,256,2,128]{4,3,2,1,0:T(2,128)S(1)}, f32[2,1,256,2,128]{4,3,2,1,0:T(2,128)}, u32[]{:S(2)}) copy-start(f32[2,1,256,2,128]{4,3,2,1,0:T(2,128)} %param.12) | copy-start | bytes 1572868
  852.7 7.4 copy-start.10
  852.7 48.4 %all-to-all-start = ((f32[2,1,256,2,128]{4,3,0,1,2:T(2,128)}), f32[2,1,256,2,128]{4,3,0,1,2:T(2,128)S(1)}, u32[]{:S(2)}, u32[]{:S(2)}) async-start(f32[2,1,256,2,128]{4,3,0,1,2:T(2,128)} %copy.228), calls=%async_computation | async-start | bytes 1048576 | tf_op jit(solution)/shard_map/all_to_all | solution.py:53
  903.1 20.0 %all-to-all-start.1 = ((f32[2,1,32,16,128]{4,2,0,1,3:T(8,128)}), f32[2,1,32,16,128]{4,2,0,1,3:T(8,128)S(1)}, u32[]{:S(2)}, u32[]{:S(2)}) async-start(f32[2,1,32,16,128]{4,2,0,1,3:T(8,128)} %copy.231), calls=%async_computation.1 | async-start | bytes 1048576 | tf_op jit(solution)/shard_map/all_to_all | solution.py:51
  909.8 0.7 copy-start.11
  910.5 0.7 copy-start.12
  923.1 1.0 copy-start
  944.1 17.7 %all-to-all-start.3 = ((f32[2,1,32,16,128]{4,2,0,1,3:T(8,128)}), f32[2,1,32,16,128]{4,2,0,1,3:T(8,128)S(1)}, u32[]{:S(2)}, u32[]{:S(2)}) async-start(f32[2,1,32,16,128]{4,2,0,1,3:T(8,128)} %copy.236), calls=%async_computation.3 | async-start | bytes 1048576 | tf_op jit(solution)/shard_map/all_to_all | solution.py:51
  963.9 1.0 copy-start.8
  965.3 14.3 %collective-permute-start = (f32[2,2,256,2,128]{4,2,3,1,0:T(8,128)S(1)}, f32[2,2,256,2,128]{4,2,3,1,0:T(8,128)S(1)}, u32[]{:S(2)}, u32[]{:S(2)}) collective-permute-start(f32[2,2,256,2,128]{4,2,3,1,0:T(8,128)S(1)} %pad_maximum_fusion), channel_id=1, source_target_pairs={{0,8},{8,16},{16,24},{24,0},{1,9},{9,17},{17,25},{25,1},{2,10},{10... | collective-permute-start | bytes 3145736 | tf_op jit(solution)/shard_map/ppermute | solution.py:16
  979.6 1.0 copy-start.7
  980.6 14.3 %collective-permute-start.1 = (f32[2,2,256,2,128]{4,2,3,1,0:T(8,128)S(1)}, f32[2,2,256,2,128]{4,2,3,1,0:T(8,128)}, u32[]{:S(2)}, u32[]{:S(2)}) collective-permute-start(f32[2,2,256,2,128]{4,2,3,1,0:T(8,128)S(1)} %collective-permute-done), channel_id=1, source_target_pairs={{0,8},{8,16},{16,24},{24,0},{1,9},{9,17},{17,25},{25,1},{2,10},{10... | collective-permute-start | bytes 3145736 | tf_op jit(solution)/shard_map/ppermute | solution.py:16
  994.9 14.5 %collective-permute-start.2 = (f32[2,2,256,2,128]{4,2,3,1,0:T(8,128)}, f32[2,2,256,2,128]{4,2,3,1,0:T(8,128)}, u32[]{:S(2)}, u32[]{:S(2)}) collective-permute-start(f32[2,2,256,2,128]{4,2,3,1,0:T(8,128)} %collective-permute-done.1), channel_id=1, source_target_pairs={{0,8},{8,16},{16,24},{24,0},{1,9},{9,17},{17,25},{25,1},{2,10},{10... | collective-permute-start | bytes 3145736 | tf_op jit(solution)/shard_map/ppermute | solution.py:16
  999.2 2.0 copy-start.1
  1012.6 2.1 copy-start.5
  1104.0 1.2 copy-start.2
  1104.0 1.4 copy-start.3
  1104.0 1.5 copy-start.6
  1108.0 14.3 %collective-permute-start.3 = (f32[2,2,256,2,128]{4,2,3,1,0:T(8,128)S(1)}, f32[2,2,256,2,128]{4,2,3,1,0:T(8,128)S(1)}, u32[]{:S(2)}, u32[]{:S(2)}) collective-permute-start(f32[2,2,256,2,128]{4,2,3,1,0:T(8,128)S(1)} %pad_maximum_fusion.1), channel_id=1, source_target_pairs={{0,8},{8,16},{16,24},{24,0},{1,9},{9,17},{17,25},{25,1},{2,10},{10... | collective-permute-start | bytes 3145736 | tf_op jit(solution)/shard_map/ppermute | solution.py:16
  1122.3 14.2 %collective-permute-start.4 = (f32[2,2,256,2,128]{4,2,3,1,0:T(8,128)S(1)}, f32[2,2,256,2,128]{4,2,3,1,0:T(8,128)S(1)}, u32[]{:S(2)}, u32[]{:S(2)}) collective-permute-start(f32[2,2,256,2,128]{4,2,3,1,0:T(8,128)S(1)} %collective-permute-done.3), channel_id=1, source_target_pairs={{0,8},{8,16},{16,24},{24,0},{1,9},{9,17},{17,25},{25,1},{2,10},{10... | collective-permute-start | bytes 3145736 | tf_op jit(solution)/shard_map/ppermute | solution.py:16
  1136.5 14.2 %collective-permute-start.5 = (f32[2,2,256,2,128]{4,2,3,1,0:T(8,128)S(1)}, f32[2,2,256,2,128]{4,2,3,1,0:T(8,128)S(1)}, u32[]{:S(2)}, u32[]{:S(2)}) collective-permute-start(f32[2,2,256,2,128]{4,2,3,1,0:T(8,128)S(1)} %collective-permute-done.4), channel_id=1, source_target_pairs={{0,8},{8,16},{16,24},{24,0},{1,9},{9,17},{17,25},{25,1},{2,10},{10... | collective-permute-start | bytes 3145736 | tf_op jit(solution)/shard_map/ppermute | solution.py:16
where the time goes:
time: 1170 us; the launch traced here: 1150 us
  loops' own time  419 us (36%)
  other arithmetic  341 us (29%)
  waiting for transfers between devices  97.2 us (8%)
  local copies, waits for them, and re-layouts  92.5 us (8%)
  blocking collectives  90.3 us (8%)
  between operations  88.8 us (8%)
  starting transfers between devices  17.2 us (1%)
    another operation x2, loops' own time, line_inverse(): lax.linalg.tridiagonal_solve(-left, 1.0 + left + right, -right, identity)  419 us
    div x9, other arithmetic, line_inverse(): lax.linalg.tridiagonal_solve(-left, 1.0 + left + right, -right, identity)  170 us
    sub x9, other arithmetic, line_inverse(): lax.linalg.tridiagonal_solve(-left, 1.0 + left + right, -right, identity)  159 us
    ppermute x6, waiting for transfers between devices, shifted(): lax.ppermute(array, axis, [(i, (i + by) % devices) for i in range(devices)])  71.4 us
    all_to_all x3, blocking collectives, column_pass(): lax.all_to_all(field, 'space', split_axis=2, concat_axis=3, tiled=True)  54.5 us
    slice x104, local copies, waits for them, and re-layouts, line_inverse(): lax.linalg.tridiagonal_solve(-left, 1.0 + left + right, -right, identity)  50.8 us
    all_to_all x2, blocking collectives, column_pass(): lax.all_to_all(solve_lines(lax.all_to_all(field, 'space', split_axis=2, c...  35.9 us
    all_to_all x2, waiting for transfers between devices, column_pass(): lax.all_to_all(solve_lines(lax.all_to_all(field, 'space', split_axis=2, c...  25.8 us
  transfers between devices with their start and end apart: 9, of which 8 were waited for; matrix products, arithmetic and copies ran while one was open for 2% of the time, Pallas kernels for 0%

commit v1 on v0

--- a/solution.py
+++ b/solution.py
@@ -1,8 +1,11 @@
+import functools
 import math
 
 import jax
 import jax.numpy as jnp
 from jax import lax
+from jax.experimental import pallas as pl
+from jax.experimental.pallas import tpu as pltpu
 from jax.sharding import PartitionSpec as P
 
 STEPS = 2
@@ -115,9 +118,400 @@
     return states
 
 
+LANES = 128
+HALO = 2 * ITERS
+MESH = pl.DeviceIdType.MESH
+
+
+def dot(a, b):
+    return jnp.dot(a, b, precision=lax.Precision.HIGHEST, preferred_element_type=jnp.float32)
+
+
+def iota(shape, axis):
+    return lax.broadcasted_iota(jnp.int32, shape, axis)
+
+
+def faces(kappa_row, n):
+    row, col = iota((n, n), 0), iota((n, n), 1)
+    own = jnp.sum(jnp.where(row == col, kappa_row, 0.0), axis=1, keepdims=True)
+    face = 0.5 * (own + kappa_row)
+    below = jnp.where(col == row - 1, face, 0.0)
+    above = jnp.where(col == row + 1, face, 0.0)
+    return (
+        jnp.sum(below, axis=1, keepdims=True),
+        jnp.sum(above, axis=1, keepdims=True),
+        below + above,
+    )
+
+
+def reduced_inverse(kappa_row, n):
+    lower, upper, _ = faces(kappa_row, n)
+    shape = (n, LANES)
+    a = jnp.broadcast_to(-lower, shape)
+    c = jnp.broadcast_to(-upper, shape)
+    b = 1.0 - a - c
+    blocks = [
+        (iota(shape, 0) == iota(shape, 1) + LANES * j).astype(jnp.float32)
+        for j in range(max(n // LANES, 1))
+    ]
+    s = 1
+    while s < n:
+        before = functools.partial(pltpu.roll, shift=s, axis=0)
+        after = functools.partial(pltpu.roll, shift=n - s, axis=0)
+        alpha = -a / before(b)
+        gamma = -c / after(b)
+        blocks = [d + alpha * before(d) + gamma * after(d) for d in blocks]
+        b = b + alpha * before(c) + gamma * after(a)
+        a, c = alpha * before(a), gamma * after(c)
+        s *= 2
+    inverse = 1.0 / b
+    return [d * inverse for d in blocks]
+
+
+def period_kernel(
+    size, u_ref, f_ref, damp_ref, kx_ref, ky_ref, kz_ref, sea_ref, phase_ref, out_ref,
+    ubuf, fbuf, pbuf, xbuf, dbuf, qbuf, obuf, rbuf, g_ref, a_ref, state, factor, source, offset_ref,
+    u_send, u_recv, f_send, f_recv, p_send, p_recv, o_send, o_recv,
+):
+    n_tm, n_sp, n_t, nx, rows, nz = size
+    count = n_tm * n_sp
+    per = count // n_t
+    chunk = nz // per
+    window = chunk + 2 * HALO
+    halves = nx // LANES
+    wrows = window * rows
+    crows = chunk * rows
+    all_rows = n_sp * wrows
+    ny = n_sp * rows
+
+    here = lax.axis_index("tm")
+    spot = lax.axis_index("space")
+    me = here * n_sp + spot
+
+    def window_start(k):
+        return jnp.minimum(jnp.maximum(k * chunk - HALO, 0), nz - window)
+
+    def window_rows(k):
+        return pl.ds(pl.multiple_of(window_start(k) * rows, 8), wrows)
+
+    def chunk_rows(k):
+        return pl.ds(pl.multiple_of(k * crows, 8), crows)
+
+    def device(index):
+        return {"tm": index // n_sp, "space": index % n_sp}
+
+    barrier = pltpu.get_barrier_semaphore()
+
+    @pl.loop(1, count)
+    def greet(offset):
+        pl.semaphore_signal(
+            barrier, inc=1, device_id=device((me + offset) % count), device_id_type=MESH
+        )
+
+    def turn(ref, buf, where):
+        for t in range(n_t):
+            for half in range(halves):
+                for y in range(rows):
+                    part = ref[t, pl.ds(half * LANES * rows + y, LANES, stride=rows), :]
+                    buf[(t, *where, half, pl.ds(y, nz, stride=rows), slice(None))] = part.T
+
+    turn(u_ref, ubuf, ())
+    turn(damp_ref, fbuf, (0,))
+    turn(f_ref, fbuf, (1,))
+    pbuf[...] = jnp.full((8, LANES), phase_ref[0].astype(jnp.float32))
+
+    my_t, my_k = me // per, me % per
+    my_start = window_start(my_k)
+
+    own_copies = [
+        pltpu.make_async_copy(
+            ubuf.at[my_t, :, window_rows(my_k), :], xbuf.at[here, spot], u_recv.at[me]
+        ),
+        pltpu.make_async_copy(
+            fbuf.at[my_t, :, :, window_rows(my_k), :], dbuf.at[spot], f_recv.at[spot]
+        ),
+        pltpu.make_async_copy(pbuf, qbuf.at[here], p_recv.at[here]),
+    ]
+
+    def send_u(offset):
+        index = (me + offset) % count
+        return pltpu.make_async_remote_copy(
+            src_ref=ubuf.at[index // per, :, window_rows(index % per), :],
+            dst_ref=xbuf.at[here, spot],
+            send_sem=u_send.at[offset],
+            recv_sem=u_recv.at[me],
+            device_id=device(index),
+            device_id_type=MESH,
+        )
+
+    def send_f(offset):
+        index = here * n_sp + (spot + offset) % n_sp
+        return pltpu.make_async_remote_copy(
+            src_ref=fbuf.at[index // per, :, :, window_rows(index % per), :],
+            dst_ref=dbuf.at[spot],
+            send_sem=f_send.at[offset],
+            recv_sem=f_recv.at[spot],
+            device_id=device(index),
+            device_id_type=MESH,
+        )
+
+    def send_p(offset):
+        return pltpu.make_async_remote_copy(
+            src_ref=pbuf,
+            dst_ref=qbuf.at[here],
+            send_sem=p_send.at[offset],
+            recv_sem=p_recv.at[here],
+            device_id={"tm": (here + offset) % n_tm, "space": spot},
+            device_id_type=MESH,
+        )
+
+    def send_o(offset):
+        index = (me + offset) % count
+        inner = pl.multiple_of((my_k * chunk - my_start) * rows, 8)
+        return pltpu.make_async_remote_copy(
+            src_ref=obuf.at[index // n_sp, index % n_sp, :, pl.ds(inner, crows), :],
+            dst_ref=rbuf.at[my_t, :, chunk_rows(my_k), :],
+            send_sem=o_send.at[offset],
+            recv_sem=o_recv.at[me],
+            device_id=device(index),
+            device_id_type=MESH,
+        )
+
+    pl.semaphore_wait(barrier, count - 1)
+
+    @pl.loop(1, n_tm)
+    def start_p(offset):
+        send_p(offset).start()
+
+    @pl.loop(1, count)
+    def start_u(offset):
+        send_u(offset).start()
+
+    @pl.loop(1, n_sp)
+    def start_f(offset):
+        send_f(offset).start()
+
+    for copy in own_copies:
+        copy.start()
+
+    for half, block in enumerate(reduced_inverse(kx_ref[...], nx)):
+        a_ref[0, :, half * LANES : (half + 1) * LANES] = block
+    a_ref[1] = dot(a_ref[0], a_ref[0])
+    q, j = iota((all_rows, ny), 0), iota((all_rows, ny), 1)
+    line = (q // wrows) * rows + q % rows
+    pick_y = (line == j).astype(jnp.float32)
+    q, j = iota((LANES, all_rows), 1), iota((LANES, all_rows), 0)
+    line = (q // wrows) * rows + q % rows
+    pick_y_back = (line == j).astype(jnp.float32)
+    big_y = dot(dot(pick_y, reduced_inverse(ky_ref[...], ny)[0]), pick_y_back)
+    _, _, beside = faces(kz_ref[...], nz)
+    identity = (iota((nz, nz), 0) == iota((nz, nz), 1)).astype(jnp.float32)
+    vertical = beside + identity * (1.0 - jnp.sum(beside, axis=1, keepdims=True))
+    q, j = iota((all_rows, nz), 0), iota((all_rows, nz), 1)
+    pick_z = (my_start + (q % wrows) // rows == j).astype(jnp.float32)
+    q, j = iota((nz, all_rows), 1), iota((nz, all_rows), 0)
+    pick_z_back = (my_start + (q % wrows) // rows == j).astype(jnp.float32)
+    g_ref[0] = big_y * dot(dot(pick_z, vertical), pick_z_back)
+    g_ref[1] = dot(g_ref[0], g_ref[0])
+    tile = (iota((nx // TILE, nx), 1) // TILE == iota((nx // TILE, nx), 0)).astype(jnp.float32)
+    sea = jnp.sum(sea_ref[...].astype(jnp.float32) * tile, axis=0, keepdims=True)
+
+    def gathered(ref, where):
+        return jnp.concatenate(
+            [ref[where(half)].reshape(all_rows, LANES) for half in range(halves)], axis=1
+        )
+
+    own_copies[1].wait()
+    own_copies[2].wait()
+
+    @pl.loop(1, n_tm)
+    def wait_p(offset):
+        index = (here + n_tm - offset) % n_tm
+        pltpu.make_async_copy(qbuf.at[index], qbuf.at[index], p_recv.at[index]).wait()
+
+    @pl.loop(1, n_sp)
+    def wait_f(offset):
+        index = (spot + n_sp - offset) % n_sp
+        pltpu.make_async_copy(dbuf.at[index], dbuf.at[index], f_recv.at[index]).wait()
+
+    source[1] = gathered(dbuf, lambda half: (slice(None), 1, half)) * sea
+    source[0] = dot(dot(g_ref[0], source[1]), a_ref[0])
+
+    @pl.loop(0, n_tm)
+    def make_factors(n):
+        log_damp = jnp.log(gathered(dbuf, lambda half: (slice(None), 0, half)))
+        phase = qbuf[n]
+        weight = 1.0 + 0.5 * jnp.cos(2.0 * math.pi * phase / PHASES)
+        first = jnp.cos(2.0 * math.pi * (phase * STEPS) / (PHASES * STEPS))
+        second = jnp.cos(2.0 * math.pi * (phase * STEPS + 1) / (PHASES * STEPS))
+
+        def wide(values):
+            return jnp.concatenate([values[:1]] * halves, axis=1)
+
+        factor[n] = jnp.exp(wide(weight) * log_damp)
+        offset_ref[n] = wide(first) * source[0] + wide(second) * source[1]
+
+    own_copies[0].wait()
+
+    @pl.loop(1, count)
+    def wait_u(offset):
+        index = (me + count - offset) % count
+        slot = xbuf.at[index // n_sp, index % n_sp]
+        pltpu.make_async_copy(slot, slot, u_recv.at[index]).wait()
+
+    @pl.loop(0, n_tm)
+    def take(n):
+        state[n] = gathered(xbuf, lambda half: (n, slice(None), half))
+
+    for iteration in range(ITERS):
+
+        @pl.loop(0, n_tm)
+        def fine(n):
+            field = state[n]
+            moved = dot(dot(g_ref[1], field), a_ref[1])
+            state[n] = moved + offset_ref[n] - factor[n] * field
+
+        product = factor[0]
+        total = state[0]
+        for n in range(1, n_tm):
+            product = factor[n] * product
+            total = factor[n] * total + state[n]
+        fresh = total / (1.0 - product)
+        for n in range(n_tm):
+            later = factor[n] * fresh + state[n]
+            state[n] = fresh
+            fresh = later
+
+    @pl.loop(0, n_tm)
+    def put(n):
+        for half in range(halves):
+            obuf[n, :, half] = state[n, :, half * LANES : (half + 1) * LANES].reshape(
+                n_sp, wrows, LANES
+            )
+
+    inner = pl.multiple_of((my_k * chunk - my_start) * rows, 8)
+    back = pltpu.make_async_copy(
+        obuf.at[here, spot, :, pl.ds(inner, crows), :],
+        rbuf.at[my_t, :, chunk_rows(my_k), :],
+        o_recv.at[me],
+    )
+
+    @pl.loop(1, count)
+    def start_o(offset):
+        send_o(offset).start()
+
+    back.start()
+    back.wait()
+
+    @pl.loop(1, count)
+    def wait_o(offset):
+        index = (me + count - offset) % count
+        slot = rbuf.at[index // per, :, chunk_rows(index % per), :]
+        pltpu.make_async_copy(slot, slot, o_recv.at[index]).wait()
+
+    for t in range(n_t):
+        for half in range(halves):
+            for y in range(rows):
+                part = rbuf[t, half, pl.ds(y, nz, stride=rows), :]
+                out_ref[t, pl.ds(half * LANES * rows + y, LANES, stride=rows), :] = part.T
+
+    @pl.loop(1, count)
+    def sent(offset):
+        send_u(offset).wait_send()
+        send_o(offset).wait_send()
+
+    @pl.loop(1, n_sp)
+    def sent_f(offset):
+        send_f(offset).wait_send()
+
+    @pl.loop(1, n_tm)
+    def sent_p(offset):
+        send_p(offset).wait_send()
+
+
+def whole_period(init_states, forcing, damp, kappa_x, kappa_y, kappa_z, sea_tiles, phases):
+    n_tm, n_sp = lax.axis_size("tm"), lax.axis_size("space")
+    n_t, _, nx, rows, nz = init_states.shape
+    count = n_tm * n_sp
+    chunk = nz // (count // n_t)
+    window = chunk + 2 * HALO
+    halves = nx // LANES
+    wrows = window * rows
+    all_rows = n_sp * wrows
+    flat = (n_t, nx * rows, nz)
+    vmem = pl.BlockSpec(memory_space=pltpu.VMEM)
+    f32 = jnp.float32
+    out = pl.pallas_call(
+        functools.partial(period_kernel, (n_tm, n_sp, n_t, nx, rows, nz)),
+        out_shape=jax.ShapeDtypeStruct(flat, f32),
+        in_specs=[vmem] * 7 + [pl.BlockSpec(memory_space=pltpu.SMEM)],
+        out_specs=vmem,
+        scratch_shapes=[
+            pltpu.VMEM((n_t, halves, nz * rows, LANES), f32),
+            pltpu.VMEM((n_t, 2, halves, nz * rows, LANES), f32),
+            pltpu.VMEM((8, LANES), f32),
+            pltpu.VMEM((n_tm, n_sp, halves, wrows, LANES), f32),
+            pltpu.VMEM((n_sp, 2, halves, wrows, LANES), f32),
+            pltpu.VMEM((n_tm, 8, LANES), f32),
+            pltpu.VMEM((n_tm, n_sp, halves, wrows, LANES), f32),
+            pltpu.VMEM((n_t, halves, nz * rows, LANES), f32),
+            pltpu.VMEM((2, all_rows, all_rows), f32),
+            pltpu.VMEM((2, nx, nx), f32),
+            pltpu.VMEM((n_tm, all_rows, nx), f32),
+            pltpu.VMEM((n_tm, all_rows, nx), f32),
+            pltpu.VMEM((2, all_rows, nx), f32),
+            pltpu.VMEM((n_tm, all_rows, nx), f32),
+            pltpu.SemaphoreType.DMA((count,)),
+            pltpu.SemaphoreType.DMA((count,)),
+            pltpu.SemaphoreType.DMA((n_sp,)),
+            pltpu.SemaphoreType.DMA((n_sp,)),
+            pltpu.SemaphoreType.DMA((n_tm,)),
+            pltpu.SemaphoreType.DMA((n_tm,)),
+            pltpu.SemaphoreType.DMA((count,)),
+            pltpu.SemaphoreType.DMA((count,)),
+        ],
+        compiler_params=pltpu.CompilerParams(
+            collective_id=0, has_side_effects=True, vmem_limit_bytes=40 * 1024 * 1024
+        ),
+    )(
+        init_states.reshape(flat),
+        forcing.reshape(flat),
+        damp.reshape(flat),
+        kappa_x[None],
+        kappa_y[None],
+        kappa_z[None],
+        sea_tiles,
+        phases,
+    )
+    return out.reshape(init_states.shape)
+
+
+def choose(init_states, forcing, damp, kappa_x, kappa_y, kappa_z, sea_tiles, phases):
+    count = lax.axis_size("tm") * lax.axis_size("space")
+    n_t, slabs, nx, rows, nz = init_states.shape
+    ny = lax.axis_size("space") * rows
+    per = count // n_t
+    fits = (
+        slabs == 1
+        and count % n_t == 0
+        and nz == LANES
+        and nx % LANES == 0
+        and nz % per == 0
+        and (nz // per * rows) % 8 == 0
+        and (HALO * rows) % 8 == 0
+        and nz // per + 2 * HALO <= nz
+        and ny <= LANES
+        and ny & (ny - 1) == 0
+        and sea_tiles.shape[1] == 1
+        and lax.axis_size("space") * (nz // per + 2 * HALO) * rows <= 512
+    )
+    run = whole_period if fits else body
+    return run(init_states, forcing, damp, kappa_x, kappa_y, kappa_z, sea_tiles, phases)
+
+
 def solution(mesh):
     return jax.shard_map(
-        body,
+        choose,
         mesh=mesh,
         in_specs=(
             P(None, "tm", None, "space", None),

time: 1170 us -> 72.4 us (0.06); the launches traced: 1150 us -> 72.1 us
  loops' own time: 419 us -> 0 us
  other arithmetic: 341 us -> 0 us
  waiting for transfers between devices: 97.2 us -> 0 us
  blocking collectives: 90.3 us -> 0 us
  between operations: 88.8 us -> 0.68 us
  local copies, waits for them, and re-layouts: 92.5 us -> 5.25 us
  Pallas kernels: 0 us -> 66.2 us
  starting transfers between devices: 17.2 us -> 0 us
    another operation x2 -> x0, loops' own time: 419 us -> none  [line_inverse(): lax.linalg.tridiagonal_solve(-left, 1.0 + left + right, -right, identity)]
    div x9 -> x0, other arithmetic: 170 us -> none  [line_inverse(): lax.linalg.tridiagonal_solve(-left, 1.0 + left + right, -right, identity)]
    sub x11 -> x0, other arithmetic: 162 us -> none  [the longest x9 159 us: line_inverse(): lax.linalg.tridiagonal_solve(-left, 1.0 + left + right, -right, identity)]
    all_to_all x5 -> x0, blocking collectives: 90.3 us -> none  [the longest x3 54.5 us: column_pass(): lax.all_to_all(field, 'space', split_axis=2, concat_axis=3, tiled=True)]
    ppermute x6 -> x0, waiting for transfers between devices: 71.4 us -> none  [shifted(): lax.ppermute(array, axis, [(i, (i + by) % devices) for i in range(devices)])]
    pallas_call x0 -> x1, Pallas kernels: none -> 66.2 us  [whole_period(): pl.pallas_call(functools.partial(period_kernel, (n_tm, n_sp, n_t, nx, row...]
    slice x111 -> x0, local copies, waits for them, and re-layouts: 62.2 us -> none  [the longest x104 50.8 us: line_inverse(): lax.linalg.tridiagonal_solve(-left, 1.0 + left + right, -right, identity)]
    all_to_all x3 -> x0, waiting for transfers between devices: 25.8 us -> none  [the longest x2 25.8 us: column_pass(): lax.all_to_all(solve_lines(lax.all_to_all(field, 'space', split_axis=2, c...]
  transfers between devices with their start and end apart: 9 -> 0, of which waited for: 8 -> 0; matrix products, arithmetic and copies ran while one was open for 2% -> 0% of each run, Pallas kernels for 0% -> 0%
where the time goes in v1:
time: 72.4 us; the launch traced here: 72.1 us
  Pallas kernels  66.2 us (91%)
  local copies, waits for them, and re-layouts  5.25 us (7%)
    pallas_call x1, Pallas kernels, whole_period(): pl.pallas_call(functools.partial(period_kernel, (n_tm, n_sp, n_t, nx, row...  66.2 us
    unnamed x16, local copies, waits for them, and re-layouts  5.25 us

profile of v1, /device:TPU:0, one launch (start us, length us, event | category | flops | bytes accessed | tf_op | source)
XLA Modules:
  0.0 72.1 jit_solution(14294045365971747612)
XLA Ops:
  0.7 0.0 copy-start.6
  0.7 0.6 copy-done.6
  1.3 0.0 copy-start.3
  1.3 0.0 copy-start.4
  1.3 0.0 copy-start.5
  1.3 0.1 copy.9.sea_ref
  1.4 0.6 copy-done.3
  2.0 0.0 copy-done.4
  2.0 0.0 copy-done.5
  2.0 0.0 copy-start
  2.0 1.0 %copy-done = f32[2,1,256,2,128]{4,3,2,1,0:T(2,128)S(1)} copy-done((f32[2,1,256,2,128]{4,3,2,1,0:T(2,128)S(1)}, f32[2,1,256,2,128]{4,3,2,1,0:T(2,128)}, u32[]{:S(2)}) %copy-start) | copy-done | bytes 524312
  3.0 0.0 copy-start.1
  3.0 1.0 %copy-done.1 = f32[2,256,2,128]{3,2,1,0:T(2,128)S(1)} copy-done((f32[2,256,2,128]{3,2,1,0:T(2,128)S(1)}, f32[2,256,2,128]{3,2,1,0:T(2,128)}, u32[]{:S(2)}) %copy-start.1) | copy-done | bytes 524312
  4.1 0.0 copy-start.2
  4.1 1.0 %copy-done.2 = f32[2,256,2,128]{3,2,1,0:T(2,128)S(1)} copy-done((f32[2,256,2,128]{3,2,1,0:T(2,128)S(1)}, f32[2,256,2,128]{3,2,1,0:T(2,128)}, u32[]{:S(2)}) %copy-start.2) | copy-done | bytes 524312
  5.1 66.2 %shard_map.82 = f32[2,512,128]{2,1,0:T(8,128)S(1)} custom-call(f32[2,512,128]{2,1,0:T(8,128)S(1)} %bitcast.10, f32[2,512,128]{2,1,0:T(8,128)S(1)} %bitcast.11, f32[2,512,128]{2,1,0:T(8,128)S(1)} %bitcast.12, f32[1,256]{1,0:T(1,128)S(1)} %bitcast.13, f32[1,16]{1,0:T(1,128)S(1)} %bitcast.14, f32[1,128]{1,0:T(1,128)S(1)} %bitcast.15, s32[16,1]{1,0:T(8,128)S(1)} %copy.9.sea_ref, ...), custom_call_target="tpu_custom_call" | custom-call | tf_op jit(solution)/shard_map/pallas_call | solution.py:444
  71.3 0.8 %copy.13 = f32[2,1,256,2,128]{4,3,2,1,0:T(2,128)} copy(f32[2,1,256,2,128]{4,3,2,1,0:T(2,128)S(1)} %bitcast.9) | data formatting | bytes 1048576
Async XLA Ops:
  0.7 0.7 copy-start.6
  1.3 0.7 copy-start.3
  1.3 0.7 copy-start.4
  1.3 0.7 copy-start.5
  2.0 1.0 %copy-start = (f32[2,1,256,2,128]{4,3,2,1,0:T(2,128)S(1)}, f32[2,1,256,2,128]{4,3,2,1,0:T(2,128)}, u32[]{:S(2)}) copy-start(f32[2,1,256,2,128]{4,3,2,1,0:T(2,128)} %param.8) | copy-start | bytes 1572868
  3.0 1.0 %copy-start.1 = (f32[2,256,2,128]{3,2,1,0:T(2,128)S(1)}, f32[2,256,2,128]{3,2,1,0:T(2,128)}, u32[]{:S(2)}) copy-start(f32[2,256,2,128]{3,2,1,0:T(2,128)} %param.9) | copy-start | bytes 1572868
  4.1 1.0 %copy-start.2 = (f32[2,256,2,128]{3,2,1,0:T(2,128)S(1)}, f32[2,256,2,128]{3,2,1,0:T(2,128)}, u32[]{:S(2)}) copy-start(f32[2,256,2,128]{3,2,1,0:T(2,128)} %param.10) | copy-start | bytes 1572868

commit v2 on v1

--- a/solution.py
+++ b/solution.py
@@ -127,6 +127,16 @@
     return jnp.dot(a, b, precision=lax.Precision.HIGHEST, preferred_element_type=jnp.float32)
 
 
+def parts(a):
+    high = a.astype(jnp.bfloat16)
+    return high, (a - high.astype(jnp.float32)).astype(jnp.bfloat16)
+
+
+def dot3(a, b):
+    once = functools.partial(jnp.dot, preferred_element_type=jnp.float32)
+    return once(a[0], b[0]) + (once(a[0], b[1]) + once(a[1], b[0]))
+
+
 def iota(shape, axis):
     return lax.broadcasted_iota(jnp.int32, shape, axis)
 
@@ -169,7 +179,8 @@
 
 
 def period_kernel(
-    size, u_ref, f_ref, damp_ref, kx_ref, ky_ref, kz_ref, sea_ref, phase_ref, out_ref,
+    size, u_hbm, f_hbm, damp_hbm, kx_hbm, ky_hbm, kz_hbm, sea_hbm, phase_ref, out_ref,
+    u_ref, f_ref, damp_ref, kx_ref, ky_ref, kz_ref, sea_ref, fetched, inverse_p, split,
     ubuf, fbuf, pbuf, xbuf, dbuf, qbuf, obuf, rbuf, g_ref, a_ref, state, factor, source, offset_ref,
     u_send, u_recv, f_send, f_recv, p_send, p_recv, o_send, o_recv,
 ):
@@ -200,6 +211,21 @@
     def device(index):
         return {"tm": index // n_sp, "space": index % n_sp}
 
+    pairs = (
+        (damp_hbm, damp_ref),
+        (f_hbm, f_ref),
+        (u_hbm, u_ref),
+        (kx_hbm, kx_ref),
+        (ky_hbm, ky_ref),
+        (kz_hbm, kz_ref),
+        (sea_hbm, sea_ref),
+    )
+    fetches = [
+        pltpu.make_async_copy(far, near, fetched.at[i]) for i, (far, near) in enumerate(pairs)
+    ]
+    for fetch in fetches:
+        fetch.start()
+
     barrier = pltpu.get_barrier_semaphore()
 
     @pl.loop(1, count)
@@ -215,9 +241,6 @@
                     part = ref[t, pl.ds(half * LANES * rows + y, LANES, stride=rows), :]
                     buf[(t, *where, half, pl.ds(y, nz, stride=rows), slice(None))] = part.T
 
-    turn(u_ref, ubuf, ())
-    turn(damp_ref, fbuf, (0,))
-    turn(f_ref, fbuf, (1,))
     pbuf[...] = jnp.full((8, LANES), phase_ref[0].astype(jnp.float32))
 
     my_t, my_k = me // per, me % per
@@ -265,34 +288,43 @@
             device_id_type=MESH,
         )
 
-    def send_o(offset):
-        index = (me + offset) % count
+    def send_o(index):
         inner = pl.multiple_of((my_k * chunk - my_start) * rows, 8)
         return pltpu.make_async_remote_copy(
             src_ref=obuf.at[index // n_sp, index % n_sp, :, pl.ds(inner, crows), :],
             dst_ref=rbuf.at[my_t, :, chunk_rows(my_k), :],
-            send_sem=o_send.at[offset],
+            send_sem=o_send.at[index],
             recv_sem=o_recv.at[me],
             device_id=device(index),
             device_id_type=MESH,
         )
 
+    fetches[0].wait()
+    turn(damp_ref, fbuf, (0,))
+    fetches[1].wait()
+    turn(f_ref, fbuf, (1,))
     pl.semaphore_wait(barrier, count - 1)
 
     @pl.loop(1, n_tm)
     def start_p(offset):
         send_p(offset).start()
 
+    @pl.loop(1, n_sp)
+    def start_f(offset):
+        send_f(offset).start()
+
+    own_copies[1].start()
+    own_copies[2].start()
+    fetches[2].wait()
+    turn(u_ref, ubuf, ())
+
     @pl.loop(1, count)
     def start_u(offset):
         send_u(offset).start()
 
-    @pl.loop(1, n_sp)
-    def start_f(offset):
-        send_f(offset).start()
-
-    for copy in own_copies:
-        copy.start()
+    own_copies[0].start()
+    for fetch in fetches[3:]:
+        fetch.wait()
 
     for half, block in enumerate(reduced_inverse(kx_ref[...], nx)):
         a_ref[0, :, half * LANES : (half + 1) * LANES] = block
@@ -314,7 +346,15 @@
     g_ref[0] = big_y * dot(dot(pick_z, vertical), pick_z_back)
     g_ref[1] = dot(g_ref[0], g_ref[0])
     tile = (iota((nx // TILE, nx), 1) // TILE == iota((nx // TILE, nx), 0)).astype(jnp.float32)
-    sea = jnp.sum(sea_ref[...].astype(jnp.float32) * tile, axis=0, keepdims=True)
+    tiles = nx // TILE
+    flags = jnp.where(
+        iota((tiles, tiles), 0) == iota((tiles, tiles), 1), sea_ref[...].astype(jnp.float32), 0.0
+    )
+    sea = jnp.sum(jnp.sum(flags, axis=1, keepdims=True) * tile, axis=0, keepdims=True)
+    g_parts, a_parts = parts(g_ref[1]), parts(a_ref[1])
+    for i in range(2):
+        split[0, i, :all_rows, :all_rows] = g_parts[i]
+        split[1, i, :nx, :nx] = a_parts[i]
 
     def gathered(ref, where):
         return jnp.concatenate(
@@ -351,43 +391,50 @@
         factor[n] = jnp.exp(wide(weight) * log_damp)
         offset_ref[n] = wide(first) * source[0] + wide(second) * source[1]
 
+    product = factor[0]
+    for n in range(1, n_tm):
+        product = factor[n] * product
+    inverse_p[...] = 1.0 / (1.0 - product)
+
+    def fine(n, field):
+        g_split = split[0, 0, :all_rows, :all_rows], split[0, 1, :all_rows, :all_rows]
+        a_split = split[1, 0, :nx, :nx], split[1, 1, :nx, :nx]
+        moved = dot3(parts(dot3(g_split, parts(field))), a_split)
+        state[n] = moved + offset_ref[n] - factor[n] * field
+
     own_copies[0].wait()
 
-    @pl.loop(1, count)
-    def wait_u(offset):
-        index = (me + count - offset) % count
-        slot = xbuf.at[index // n_sp, index % n_sp]
-        pltpu.make_async_copy(slot, slot, u_recv.at[index]).wait()
-
-    @pl.loop(0, n_tm)
-    def take(n):
-        state[n] = gathered(xbuf, lambda half: (n, slice(None), half))
-
-    for iteration in range(ITERS):
-
-        @pl.loop(0, n_tm)
-        def fine(n):
-            field = state[n]
-            moved = dot(dot(g_ref[1], field), a_ref[1])
-            state[n] = moved + offset_ref[n] - factor[n] * field
-
-        product = factor[0]
-        total = state[0]
+    @pl.loop(1, n_tm + 1)
+    def fine_first(turned):
+        n = (here + n_tm - turned) % n_tm
+
+        @pl.loop(0, n_sp)
+        def wait_u(r):
+            @pl.when(n * n_sp + r != me)
+            def _():
+                slot = xbuf.at[n, r]
+                pltpu.make_async_copy(slot, slot, u_recv.at[n * n_sp + r]).wait()
+
+        fine(n, gathered(xbuf, lambda half: (n, slice(None), half)))
+
+    def solve(r, keep):
+        block = pl.ds(pl.multiple_of(r * wrows, 8), wrows)
+        factors = [factor[n, block, :] for n in range(n_tm)]
+        offsets = [state[n, block, :] for n in range(n_tm)]
+        total = offsets[0]
         for n in range(1, n_tm):
-            product = factor[n] * product
-            total = factor[n] * total + state[n]
-        fresh = total / (1.0 - product)
+            total = factors[n] * total + offsets[n]
+        fresh = total * inverse_p[block, :]
         for n in range(n_tm):
-            later = factor[n] * fresh + state[n]
-            state[n] = fresh
-            fresh = later
-
-    @pl.loop(0, n_tm)
-    def put(n):
-        for half in range(halves):
-            obuf[n, :, half] = state[n, :, half * LANES : (half + 1) * LANES].reshape(
-                n_sp, wrows, LANES
-            )
+            keep(n, block, fresh)
+            fresh = factors[n] * fresh + offsets[n]
+
+    def keep_state(n, block, values):
+        state[n, block, :] = values
+
+    for iteration in range(1, ITERS):
+        pl.loop(0, n_sp)(lambda r: solve(r, keep_state))
+        pl.loop(0, n_tm)(lambda n: fine(n, state[n]))
 
     inner = pl.multiple_of((my_k * chunk - my_start) * rows, 8)
     back = pltpu.make_async_copy(
@@ -396,20 +443,33 @@
         o_recv.at[me],
     )
 
-    @pl.loop(1, count)
-    def start_o(offset):
-        send_o(offset).start()
+    @pl.loop(1, n_sp + 1)
+    def solve_last(turned):
+        r = (spot + turned) % n_sp
+
+        def keep_out(n, block, values):
+            for half in range(halves):
+                obuf[n, r, half] = values[:, half * LANES : (half + 1) * LANES]
+
+        solve(r, keep_out)
+        for n in range(n_tm):
+
+            @pl.when(n * n_sp + r != me)
+            def _():
+                send_o(n * n_sp + r).start()
 
     back.start()
     back.wait()
 
-    @pl.loop(1, count)
-    def wait_o(offset):
-        index = (me + count - offset) % count
-        slot = rbuf.at[index // per, :, chunk_rows(index % per), :]
-        pltpu.make_async_copy(slot, slot, o_recv.at[index]).wait()
-
     for t in range(n_t):
+
+        @pl.loop(t * per, (t + 1) * per)
+        def wait_o(index):
+            @pl.when(index != me)
+            def _():
+                slot = rbuf.at[t, :, chunk_rows(index % per), :]
+                pltpu.make_async_copy(slot, slot, o_recv.at[index]).wait()
+
         for half in range(halves):
             for y in range(rows):
                 part = rbuf[t, half, pl.ds(y, nz, stride=rows), :]
@@ -418,7 +478,7 @@
     @pl.loop(1, count)
     def sent(offset):
         send_u(offset).wait_send()
-        send_o(offset).wait_send()
+        send_o((me + offset) % count).wait_send()
 
     @pl.loop(1, n_sp)
     def sent_f(offset):
@@ -444,9 +504,19 @@
     out = pl.pallas_call(
         functools.partial(period_kernel, (n_tm, n_sp, n_t, nx, rows, nz)),
         out_shape=jax.ShapeDtypeStruct(flat, f32),
-        in_specs=[vmem] * 7 + [pl.BlockSpec(memory_space=pltpu.SMEM)],
+        in_specs=[pl.BlockSpec(memory_space=pltpu.HBM)] * 7 + [pl.BlockSpec(memory_space=pltpu.SMEM)],
         out_specs=vmem,
         scratch_shapes=[
+            pltpu.VMEM(flat, f32),
+            pltpu.VMEM(flat, f32),
+            pltpu.VMEM(flat, f32),
+            pltpu.VMEM((1, nx), f32),
+            pltpu.VMEM((1, kappa_y.shape[0]), f32),
+            pltpu.VMEM((1, nz), f32),
+            pltpu.VMEM((1, sea_tiles.shape[0]), jnp.int32),
+            pltpu.SemaphoreType.DMA((7,)),
+            pltpu.VMEM((all_rows, nx), f32),
+            pltpu.VMEM((2, 2, max(all_rows, nx), max(all_rows, nx)), jnp.bfloat16),
             pltpu.VMEM((n_t, halves, nz * rows, LANES), f32),
             pltpu.VMEM((n_t, 2, halves, nz * rows, LANES), f32),
             pltpu.VMEM((8, LANES), f32),
@@ -471,7 +541,7 @@
             pltpu.SemaphoreType.DMA((count,)),
         ],
         compiler_params=pltpu.CompilerParams(
-            collective_id=0, has_side_effects=True, vmem_limit_bytes=40 * 1024 * 1024
+            collective_id=0, has_side_effects=True, vmem_limit_bytes=63 * 1024 * 1024
         ),
     )(
         init_states.reshape(flat),
@@ -480,7 +550,7 @@
         kappa_x[None],
         kappa_y[None],
         kappa_z[None],
-        sea_tiles,
+        sea_tiles.reshape(1, -1),
         phases,
     )
     return out.reshape(init_states.shape)

time: 72.4 us -> 62.8 us (0.87)
  the two profiles are of different devices: /device:TPU:0 before, /device:TPU:15 now
where the time goes in v2:
time: 62.8 us; the launch traced here: 62.6 us
  Pallas kernels  60.1 us (96%)
  local copies, waits for them, and re-layouts  1.87 us (3%)
  between operations  0.66 us (1%)
    pallas_call x1, Pallas kernels, whole_period(): pl.pallas_call(functools.partial(period_kernel, (n_tm, n_sp, n_t, nx, row...  60.1 us
    unnamed x1, local copies, waits for them, and re-layouts  1.87 us

profile of v2, /device:TPU:15, one launch (start us, length us, event | category | flops | bytes accessed | tf_op | source)
XLA Modules:
  0.0 62.6 jit_solution(3269950510135758308)
XLA Ops:
  0.7 60.1 %shard_map.82 = f32[2,512,128]{2,1,0:T(8,128)} custom-call(f32[2,512,128]{2,1,0:T(8,128)} %bitcast.11, f32[2,512,128]{2,1,0:T(8,128)} %bitcast.12, f32[2,512,128]{2,1,0:T(8,128)} %bitcast.13, f32[1,256]{1,0:T(1,128)} %bitcast.14, f32[1,16]{1,0:T(1,128)} %bitcast.15, f32[1,128]{1,0:T(1,128)} %bitcast.16, s32[1,16]{1,0:T(1,128)} %bitcast.17, s32[1]{0:T(128)S(6)} %copy.11.phase_ref), custom_call_target="tpu_custom_call" | custom-call | tf_op jit(solution)/shard_map/pallas_call | solution.py:504
  60.8 1.9 %copy.12 = f32[2,1,256,2,128]{4,3,2,1,0:T(2,128)} copy(f32[2,1,256,2,128]{4,3,2,1,0:T(2,128)} %bitcast.10) | data formatting | bytes 1048576

commit v3 on v2

--- a/solution.py
+++ b/solution.py
@@ -180,7 +180,7 @@
 
 def period_kernel(
     size, u_hbm, f_hbm, damp_hbm, kx_hbm, ky_hbm, kz_hbm, sea_hbm, phase_ref, out_ref,
-    u_ref, f_ref, damp_ref, kx_ref, ky_ref, kz_ref, sea_ref, fetched, inverse_p, split,
+    u_ref, f_ref, damp_ref, kx_ref, ky_ref, kz_ref, sea_ref, fetched, inverse_p, split, ends,
     ubuf, fbuf, pbuf, xbuf, dbuf, qbuf, obuf, rbuf, g_ref, a_ref, state, factor, source, offset_ref,
     u_send, u_recv, f_send, f_recv, p_send, p_recv, o_send, o_recv,
 ):
@@ -417,10 +417,17 @@
 
         fine(n, gathered(xbuf, lambda half: (n, slice(None), half)))
 
-    def solve(r, keep):
+    def fine_rows(n, block):
+        field = state[n]
+        g_split = split[0, 0, block, :all_rows], split[0, 1, block, :all_rows]
+        a_split = split[1, 0, :nx, :nx], split[1, 1, :nx, :nx]
+        moved = dot3(parts(dot3(g_split, parts(field))), a_split)
+        ends[n, block, :] = moved + offset_ref[n, block, :] - factor[n, block, :] * state[n, block, :]
+
+    def solve(r, held, keep):
         block = pl.ds(pl.multiple_of(r * wrows, 8), wrows)
         factors = [factor[n, block, :] for n in range(n_tm)]
-        offsets = [state[n, block, :] for n in range(n_tm)]
+        offsets = [held[n, block, :] for n in range(n_tm)]
         total = offsets[0]
         for n in range(1, n_tm):
             total = factors[n] * total + offsets[n]
@@ -433,8 +440,9 @@
         state[n, block, :] = values
 
     for iteration in range(1, ITERS):
-        pl.loop(0, n_sp)(lambda r: solve(r, keep_state))
-        pl.loop(0, n_tm)(lambda n: fine(n, state[n]))
+        pl.loop(0, n_sp)(lambda r: solve(r, state, keep_state))
+        if iteration < ITERS - 1:
+            pl.loop(0, n_tm)(lambda n: fine(n, state[n]))
 
     inner = pl.multiple_of((my_k * chunk - my_start) * rows, 8)
     back = pltpu.make_async_copy(
@@ -443,20 +451,29 @@
         o_recv.at[me],
     )
 
-    @pl.loop(1, n_sp + 1)
-    def solve_last(turned):
-        r = (spot + turned) % n_sp
-
-        def keep_out(n, block, values):
-            for half in range(halves):
-                obuf[n, r, half] = values[:, half * LANES : (half + 1) * LANES]
-
-        solve(r, keep_out)
+    near_half = spot // (n_sp // 2)
+
+    @pl.loop(1, 3)
+    def last_half(turned_half):
+        part = (near_half + turned_half) % 2
+        block = pl.ds(pl.multiple_of(part * (all_rows // 2), 16), all_rows // 2)
         for n in range(n_tm):
-
-            @pl.when(n * n_sp + r != me)
-            def _():
-                send_o(n * n_sp + r).start()
+            fine_rows(n, block)
+
+        @pl.loop(1, n_sp // 2 + 1)
+        def solve_last(turned):
+            r = part * (n_sp // 2) + (spot + turned) % (n_sp // 2)
+
+            def keep_out(n, rows_block, values):
+                for half in range(halves):
+                    obuf[n, r, half] = values[:, half * LANES : (half + 1) * LANES]
+
+            solve(r, ends, keep_out)
+            for n in range(n_tm):
+
+                @pl.when(n * n_sp + r != me)
+                def _():
+                    send_o(n * n_sp + r).start()
 
     back.start()
     back.wait()
@@ -517,6 +534,7 @@
             pltpu.SemaphoreType.DMA((7,)),
             pltpu.VMEM((all_rows, nx), f32),
             pltpu.VMEM((2, 2, max(all_rows, nx), max(all_rows, nx)), jnp.bfloat16),
+            pltpu.VMEM((n_tm, all_rows, nx), f32),
             pltpu.VMEM((n_t, halves, nz * rows, LANES), f32),
             pltpu.VMEM((n_t, 2, halves, nz * rows, LANES), f32),
             pltpu.VMEM((8, LANES), f32),
@@ -573,6 +591,7 @@
         and ny <= LANES
         and ny & (ny - 1) == 0
         and sea_tiles.shape[1] == 1
+        and lax.axis_size("space") % 2 == 0
         and lax.axis_size("space") * (nz // per + 2 * HALO) * rows <= 512
     )
     run = whole_period if fits else body

time: 62.8 us -> 62.2 us (level)
  the two profiles are of different devices: /device:TPU:15 before, /device:TPU:0 now
where the time goes in v3:
time: 62.2 us; the launch traced here: 62 us
  Pallas kernels  59.5 us (96%)
  local copies, waits for them, and re-layouts  1.87 us (3%)
  between operations  0.66 us (1%)
    pallas_call x1, Pallas kernels, whole_period(): pl.pallas_call(functools.partial(period_kernel, (n_tm, n_sp, n_t, nx, row...  59.5 us
    unnamed x1, local copies, waits for them, and re-layouts  1.87 us

profile of v3, /device:TPU:0, one launch (start us, length us, event | category | flops | bytes accessed | tf_op | source)
XLA Modules:
  0.0 62.0 jit_solution(17281524028517046686)
XLA Ops:
  0.7 59.5 %shard_map.82 = f32[2,512,128]{2,1,0:T(8,128)} custom-call(f32[2,512,128]{2,1,0:T(8,128)} %bitcast.11, f32[2,512,128]{2,1,0:T(8,128)} %bitcast.12, f32[2,512,128]{2,1,0:T(8,128)} %bitcast.13, f32[1,256]{1,0:T(1,128)} %bitcast.14, f32[1,16]{1,0:T(1,128)} %bitcast.15, f32[1,128]{1,0:T(1,128)} %bitcast.16, s32[1,16]{1,0:T(1,128)} %bitcast.17, s32[1]{0:T(128)S(6)} %copy.11.phase_ref), custom_call_target="tpu_custom_call" | custom-call | tf_op jit(solution)/shard_map/pallas_call | solution.py:521
  60.1 1.9 %copy.12 = f32[2,1,256,2,128]{4,3,2,1,0:T(2,128)} copy(f32[2,1,256,2,128]{4,3,2,1,0:T(2,128)} %bitcast.10) | data formatting | bytes 1048576
